TPU v7x, 32 devices: a whole 2x2x4 slice. The times are simulated.
32 devices in a mesh: groups: 2 (over y), owners: 4 (over z), inner: 2 (over x), sub: 2 (over core).
Axes of the slice: x: 2, y: 2, z: 4, core: 2. Of those that a mesh axis runs over, the one named last changes fastest.
Arguments:
- embeddings: bfloat16 [16384, 4096], P(('groups', 'owners', 'inner'), 'sub'), parts along dimension 0, may hold values from -6 to 6
- pca_basis: bfloat16 [4096, 256], P('sub', 'inner'), may hold values from -0.09375 to 0.09375
- assignment: int32 [16384, 1], P(('groups', 'owners', 'inner', 'sub')), parts along dimension 0, may hold values from 0 to 31; in each aligned block of 512 rows (0 to 511, 512 to 1023, ...) at most 32 rows name the same one
- row_stamp: int32 [16384], P(('groups', 'owners', 'inner', 'sub')), parts along dimension 0, may hold values from 0 to 8191, each once
Outputs:
- similarity: float32 [16384], P(('groups', 'owners', 'inner', 'sub')), parts along dimension 0
- centroid: float32 [64, 256], P(('groups', 'owners', 'inner'), 'sub'), parts along dimension 0
There are 2 independent parts, one for each index of `groups`. A program takes and returns all parts, laid end to end along the dimension named above; an argument that names none is the same for every part. Nothing has to cross between parts.
Inputs may be any that keep to these rules, and one draw needn't show every extreme that they name: `assignment`: among the 512 documents of one device no cluster is named more than 32 times; some cluster is named exactly 32 times by some device. `row_stamp`: A permutation of the documents.
All inputs are finite; a program needn't handle non-finite values.
Results may differ from a plain program's by a relative error of at most 0.0029.
Values may be sent and summed in bfloat16 or wider, within the bound.
A program may use at most 64 MiB of HBM per device.

v0:
```python
import jax
import jax.numpy as jnp
from jax import lax
from jax.sharding import PartitionSpec as P

KDEV = 8


EPS = 1e-06
SENTINEL = 1073741824


def key_fold(queries, query_stamp, highest, piece):
    key_rows, key_stamp = piece
    groups = queries.shape[0]
    key_rows = jnp.swapaxes(key_rows, 0, 1).reshape(groups, -1, key_rows.shape[-1])
    key_stamp = jnp.swapaxes(key_stamp, 0, 1).reshape(groups, -1)
    scores = jnp.einsum("kqp,knp->kqn", queries, key_rows, preferred_element_type=jnp.float32)
    earlier = key_stamp[:, None, :] < query_stamp[:, :, None]
    return jnp.maximum(highest, jnp.max(jnp.where(earlier, scores, -1.0), axis=2))


def as_queries(incoming, incoming_stamp):
    groups = incoming.shape[1]
    queries = jnp.swapaxes(incoming, 0, 1).reshape(groups, -1, incoming.shape[-1])
    query_stamp = jnp.swapaxes(incoming_stamp, 0, 1).reshape(groups, -1)
    return (queries, query_stamp)


def per_device(embeddings, pca_basis, assignment, row_stamp):
    full_basis = lax.all_gather(pca_basis, "inner", axis=1, tiled=True)
    row_count = assignment.shape[0]
    projected = lax.psum_scatter(
        jnp.dot(embeddings, full_basis, preferred_element_type=jnp.float32),
        "sub",
        scatter_dimension=0,
        tiled=True,
    )
    unit = (
        projected * lax.rsqrt(jnp.sum(projected * projected, axis=1, keepdims=True) + EPS)
    ).astype(jnp.bfloat16)
    features = unit.shape[1]
    owners_n = lax.axis_size("owners")
    inner_n = lax.axis_size("inner")
    sub_n = lax.axis_size("sub")
    clusters = KDEV * owners_n
    slot_count = max(2, 2 * row_count // clusters)
    local_count = KDEV // inner_n
    labels = assignment[:, 0]
    one_hot = (labels[:, None] == jnp.arange(clusters, dtype=jnp.int32)[None, :]).astype(jnp.int32)
    before = jnp.cumsum(one_hot, axis=0) - one_hot
    rank = jnp.sum(before * one_hot, axis=1)
    position = labels * slot_count + rank
    source = (
        jnp.full((clusters * slot_count,), row_count, jnp.int32)
        .at[position]
        .set(jnp.arange(row_count, dtype=jnp.int32))
    )
    padded_unit = jnp.concatenate([unit, jnp.zeros((1, features), jnp.bfloat16)], axis=0)
    padded_stamp = jnp.concatenate([row_stamp, jnp.full((1,), SENTINEL, jnp.int32)])
    outgoing = padded_unit[source]
    outgoing_stamp = padded_stamp[source]
    incoming, incoming_stamp = (
        lax.all_to_all(
            outgoing.reshape(owners_n, KDEV * slot_count, features),
            "owners",
            split_axis=0,
            concat_axis=0,
            tiled=True,
        ),
        lax.all_to_all(
            outgoing_stamp.reshape(owners_n, KDEV * slot_count),
            "owners",
            split_axis=0,
            concat_axis=0,
            tiled=True,
        ),
    )
    incoming = incoming.reshape(owners_n, KDEV, slot_count, features)
    incoming_stamp = incoming_stamp.reshape(owners_n, KDEV, slot_count)
    queries, query_stamp = as_queries(incoming, incoming_stamp)
    start_best = jnp.full(query_stamp.shape, -1.0, jnp.float32)
    highest = key_fold(
        queries,
        query_stamp,
        start_best,
        (
            lax.all_gather(incoming, ("inner", "sub"), axis=0, tiled=True),
            lax.all_gather(incoming_stamp, ("inner", "sub"), axis=0, tiled=True),
        ),
    )
    answer = jnp.swapaxes(highest.reshape(KDEV, owners_n, slot_count), 0, 1).reshape(
        owners_n, KDEV * slot_count
    )
    returned = lax.all_to_all(answer, "owners", split_axis=0, concat_axis=0, tiled=True)
    partial_value = jnp.sum(incoming, axis=(0, 2), dtype=jnp.float32)
    half = features // sub_n
    arranged = jnp.transpose(
        partial_value.reshape(inner_n, local_count, sub_n, half), (0, 2, 1, 3)
    ).reshape(inner_n * sub_n * local_count, half)
    own_sums = lax.psum_scatter(arranged, ("inner", "sub"), scatter_dimension=0, tiled=True)
    similarity = returned.reshape(-1)[position]
    squares = lax.psum(jnp.sum(own_sums * own_sums, axis=1), "sub")
    centroid = own_sums * lax.rsqrt(squares[:, None] / features + EPS)
    return (similarity, centroid)


def solution(mesh):
    in_specs = (
        P(("groups", "owners", "inner"), "sub"),
        P("sub", "inner"),
        P(("groups", "owners", "inner", "sub"), None),
        P(("groups", "owners", "inner", "sub")),
    )
    out_specs = (P(("groups", "owners", "inner", "sub")), P(("groups", "owners", "inner"), "sub"))
    return jax.shard_map(
        per_device, mesh=mesh, in_specs=in_specs, out_specs=out_specs, check_vma=False
    )
```

profile of v0, /device:TPU:0, one launch (start us, length us, event | category | flops | bytes accessed | tf_op | source)
XLA Modules:
  0.0 128.4 jit_solution(16432663410292329869)
XLA Ops:
  7.2 0.0 all-gather.3.cloned.1.call-start
  7.2 0.7 all-gather.3.cloned.1.call-update
  7.9 0.0 copy-start.1
  7.9 0.0 reduce-scatter.2.cloned.1.call-start
  8.0 25.6 %all-gather.3.cloned.1.call-done = bf16[2048,256]{1,0:T(8,128)(2,1)} async-done(((bf16[2048,128]{1,0:T(8,128)(2,1)}), bf16[2048,256]{1,0:T(8,128)(2,1)}) %all-gather.3.cloned.1.call-update) | async-done | bytes 1048592 | tf_op jit(solution)/shard_map/all_gather | solution.py:31
  33.5 4.7 %fusion.7 = f32[1024,256]{1,0:T(8,128)} fusion(bf16[1024,2048]{1,0:T(8,128)(2,1)} %param.4, bf16[2048,256]{1,0:T(8,128)(2,1)} %all-gather.3.cloned.1.call-done), kind=kOutput, calls=%fused_computation.30 | convolution fusion | flops 1073741824 | bytes 6291456 | tf_op jit(solution)/shard_map/dot_general | solution.py:34
  38.3 0.0 reduce-scatter.2.cloned.1.call-update
  38.3 0.0 all-gather.5.cloned.1.call-start
  38.3 0.0 copy-done.1
  38.4 1.2 reduce-window.6
  39.5 0.2 slice_reduce_fusion
  39.8 0.1 fusion.2
  39.9 2.4 %scatter_custom_fusion = s32[1024]{0:T(1024)S(1)} fusion(s32[512]{0:T(512)S(1)} %bitcast.58, s32[512]{0:T(512)S(1)} %iota.11, s32[]{:T(128)} %constant.13.clone.1), kind=kCustom, calls=%fused_computation.26 | custom fusion | bytes 4100 | tf_op jit(solution)/shard_map/scatter | solution.py:57
  42.4 4.6 %reduce-scatter.2.cloned.1.call-done = f32[512,256]{1,0:T(8,128)} async-done(((f32[1024,256]{1,0:T(8,128)}), f32[512,256]{1,0:T(8,128)}) %reduce-scatter.2.cloned.1.call-update) | async-done | bytes 524304 | tf_op jit(solution)/shard_map/reduce_scatter | solution.py:33
  47.0 1.2 multiply_reduce_fusion
  48.2 1.2 multiply_convert_fusion
  49.4 0.0 copy-start.2
  49.4 3.9 %gather_fusion.1 = bf16[1024,256]{1,0:T(8,128)(2,1)S(1)} fusion(bf16[513,256]{1,0:T(8,128)(2,1)S(1)} %concatenate.7, s32[1024]{0:T(1024)S(1)} %fusion.4), kind=kCustom, calls=%fused_computation.1 | custom fusion | bytes 1052672 | tf_op jit(solution)/shard_map/gather | solution.py:61
  53.4 19.7 %all_to_all.24 = bf16[4,256,256]{2,1,0:T(8,128)(2,1)} all-to-all(bf16[4,256,256]{2,1,0:T(8,128)(2,1)S(1)} %bitcast.49), channel_id=1, replica_groups=mesh['groups'=2,'owners'=4,'inner'=2,'sub'=2] {'owners'}, dimensions={0} | all-to-all | bytes 1048576 | tf_op jit(solution)/shard_map/all_to_all | solution.py:64
  73.1 0.0 all-gather.5.cloned.1.call-update
  73.1 0.0 copy-done.2
  73.1 0.0 copy-start.3
  73.1 0.0 copy-start
  73.1 8.8 %gather_fusion = s32[1024]{0:T(1024)} fusion(s32[513]{0:T(1024)S(1)} %pad_add_fusion, s32[1024]{0:T(1024)S(1)} %fusion.4), kind=kCustom, calls=%fused_computation | custom fusion | bytes 12288 | tf_op jit(solution)/shard_map/gather | solution.py:62
  81.9 3.2 %all-to-all-start = ((s32[4,1,256]{2,1,0:T(1,128)}), s32[4,1,256]{2,1,0:T(1,128)S(1)}, u32[]{:S(2)}, u32[]{:S(2)}) async-start(s32[4,1,256]{2,1,0:T(1,128)} %bitcast.5), calls=%async_computation | async-start | bytes 8192 | tf_op jit(solution)/shard_map/all_to_all | solution.py:71
  85.2 0.0 copy-done.3
  85.2 0.6 dynamic-slice
  86.4 4.3 %all-to-all-done = s32[4,1,256]{2,1,0:T(1,128)S(1)} async-done(((s32[4,1,256]{2,1,0:T(1,128)}), s32[4,1,256]{2,1,0:T(1,128)S(1)}, u32[]{:S(2)}, u32[]{:S(2)}) %all-to-all-start) | async-done | bytes 4128 | tf_op jit(solution)/shard_map/all_to_all | solution.py:71
  90.7 0.1 reshape.73
  90.8 5.2 %all_gather.9 = s32[16,8,32]{2,1,0:T(8,128)S(1)} all-gather(s32[4,8,32]{2,1,0:T(8,128)S(1)} %reshape.73), channel_id=1, replica_groups=mesh['groups'=2,'owners'=4,'inner'=2,'sub'=2] {'inner','sub'}, dimensions={0}, use_global_device_ids=true | all-gather | bytes 20480 | tf_op jit(solution)/shard_map/all_gather | solution.py:89
  96.0 0.1 lt.28
  96.1 0.0 copy-done
  96.2 0.1 convert_reduce_fusion
  96.3 7.2 %all-reduce.1 = f32[16,128]{1,0:T(8,128)S(1)} all-reduce(f32[16,128]{1,0:T(8,128)S(1)} %bitcast.55), channel_id=3, replica_groups=mesh['groups'=2,'owners'=4,'inner'=2,'sub'=2] {'inner','sub'}, use_global_device_ids=true, to_apply=%region_9.10.clone | all-reduce | flops 2048 | bytes 16384
  103.5 0.1 multiply_reduce_fusion.1
  103.6 0.1 lt.30
  103.7 2.4 %psum.7 = f32[4]{0:T(128)S(1)} all-reduce(f32[4]{0:T(128)S(1)} %multiply_reduce_fusion.1), channel_id=1, replica_groups=mesh['groups'=2,'owners'=4,'inner'=2,'sub'=2] {'sub'}, use_global_device_ids=true, to_apply=%region_11.12 | all-reduce | flops 4 | bytes 32 | tf_op jit(solution)/shard_map/psum | solution.py:103
  106.2 0.0 all-gather.5.cloned.1.call-done
  106.2 1.8 %copy.28 = bf16[8,16,32,256]{3,2,1,0:T(8,128)(2,1)S(1)} copy(bf16[8,16,32,256]{3,2,0,1:T(8,128)(2,1)} %bitcast.47) | data formatting | bytes 4194304 | tf_op jit(solution)/shard_map/transpose | solution.py:16
  108.0 0.9 select_reduce_fusion
  108.9 0.1 max_broadcast_in_dim.8
  109.0 0.7 all_to_all.20
  109.7 3.2 %all-to-all-start.2 = ((f32[4,1,256]{2,1,0:T(1,128)}), f32[4,1,256]{2,1,0:T(1,128)S(1)}, u32[]{:S(2)}, u32[]{:S(2)}) async-start(f32[4,1,256]{2,1,0:T(1,128)} %all_to_all.20), calls=%async_computation.3 | async-start | bytes 8192 | tf_op jit(solution)/shard_map/all_to_all | solution.py:95
  112.9 0.7 dynamic-slice_multiply_fusion
  113.6 4.9 %all-to-all-done.2 = f32[4,1,256]{2,1,0:T(1,128)S(1)} async-done(((f32[4,1,256]{2,1,0:T(1,128)}), f32[4,1,256]{2,1,0:T(1,128)S(1)}, u32[]{:S(2)}, u32[]{:S(2)}) %all-to-all-start.2) | async-done | bytes 4128 | tf_op jit(solution)/shard_map/all_to_all | solution.py:95
  118.5 3.4 %gather_fusion.2 = f32[512]{0:T(512)} fusion(f32[1024]{0:T(1024)S(1)} %bitcast.44, s32[1024]{0:T(1024)S(1)} %pad_clamp_fusion), kind=kCustom, calls=%fused_computation.2 | custom fusion | bytes 6144 | tf_op jit(solution)/shard_map/gather | solution.py:102
  (20 shorter events, 0.2 us)
Async XLA Ops:
  7.2 26.4 %all-gather.3.cloned.1.call-start = ((), (), s32[]{:S(2)}) async-start(), calls=%async_computation.4 | async-start | bytes 1572864 | tf_op jit(solution)/shard_map/all_gather | solution.py:31
  7.9 30.4 %copy-start.1 = (s32[512,1]{0,1:T(1,128)S(1)}, s32[512,1]{0,1:T(1,128)}, u32[]{:S(2)}) copy-start(s32[512,1]{0,1:T(1,128)} %param.6) | copy-start | bytes 6148
  7.9 39.1 %reduce-scatter.2.cloned.1.call-start = ((), (), s32[]{:S(2)}) async-start(), calls=%async_computation.5 | async-start | bytes 1572864 | tf_op jit(solution)/shard_map/reduce_scatter | solution.py:33
  38.3 67.9 %all-gather.5.cloned.1.call-start = ((), (), s32[]{:S(2)}) async-start(), calls=%async_computation.6 | async-start | bytes 2621440 | tf_op jit(solution)/shard_map/all_gather | solution.py:88
  49.4 23.7 %copy-start.2 = (s32[512]{0:T(512)S(1)}, s32[512]{0:T(512)}, u32[]{:S(2)}) copy-start(s32[512]{0:T(512)} %param.7) | copy-start | bytes 6148
  73.1 12.0 %copy-start.3 = (u32[32]{0:T(128)S(1)}, u32[32]{0:T(128)}, u32[]{:S(2)}) copy-start(u32[32]{0:T(128)} %constant.37) | copy-start | bytes 388
  73.1 23.0 %copy-start = (bf16[4,256,256]{2,1,0:T(8,128)(2,1)S(1)}, bf16[4,256,256]{2,1,0:T(8,128)(2,1)}, u32[]{:S(2)}) copy-start(bf16[4,256,256]{2,1,0:T(8,128)(2,1)} %all_to_all.24) | copy-start | bytes 1572868
  81.9 8.8 %all-to-all-start = ((s32[4,1,256]{2,1,0:T(1,128)}), s32[4,1,256]{2,1,0:T(1,128)S(1)}, u32[]{:S(2)}, u32[]{:S(2)}) async-start(s32[4,1,256]{2,1,0:T(1,128)} %bitcast.5), calls=%async_computation | async-start | bytes 8192 | tf_op jit(solution)/shard_map/all_to_all | solution.py:71
  109.7 8.8 %all-to-all-start.2 = ((f32[4,1,256]{2,1,0:T(1,128)}), f32[4,1,256]{2,1,0:T(1,128)S(1)}, u32[]{:S(2)}, u32[]{:S(2)}) async-start(f32[4,1,256]{2,1,0:T(1,128)} %all_to_all.20), calls=%async_computation.3 | async-start | bytes 8192 | tf_op jit(solution)/shard_map/all_to_all | solution.py:95
Sparse Core Ops, SparseCore 0:
  9.5 23.9 all-gather.2
  38.4 8.5 reduce-scatter.1
  73.2 21.6 all-gather.4
where the time goes:
time: 129 us; the launch traced here: 128 us
  waiting for transfers between devices  40.1 us (31%)
  blocking collectives  34.6 us (27%)
  local copies, waits for them, and re-layouts  22.3 us (17%)
  between operations  14.6 us (11%)
  starting transfers between devices  6.59 us (5%)
  matrix products  5.64 us (4%)
  other arithmetic  4.63 us (4%)
    all_gather x1, waiting for transfers between devices, per_device(): full_basis = lax.all_gather(pca_basis, 'inner', axis=1, tiled=True)  25.6 us
    all_to_all x1, blocking collectives, per_device(): lax.all_to_all(outgoing.reshape(owners_n, KDEV * slot_count, features), '...  19.7 us
    gather x1, local copies, waits for them, and re-layouts, per_device(): outgoing_stamp = padded_stamp[source]  8.77 us
    unnamed x1, blocking collectives  7.19 us
    all_gather x1, blocking collectives, per_device(): lax.all_gather(incoming_stamp, ('inner', 'sub'), axis=0, tiled=True)  5.23 us
    all_to_all x1, waiting for transfers between devices, per_device(): lax.all_to_all(answer, 'owners', split_axis=0, concat_axis=0, tiled=True)  4.89 us
    dot_general x1, matrix products, per_device(): jnp.dot(embeddings, full_basis, preferred_element_type=jnp.float32)  4.73 us
    reduce_scatter x1, waiting for transfers between devices, per_device(): lax.psum_scatter(jnp.dot(embeddings, full_basis, preferred_element_type=j...  4.61 us
  transfers between devices with their start and end apart: 5, of which 4 were waited for; matrix products, arithmetic and copies ran while one was open for 11% of the time, Pallas kernels for 0%

commit v1 on v0

--- a/solution.py
+++ b/solution.py
@@ -1,6 +1,10 @@
+import functools
+
 import jax
 import jax.numpy as jnp
 from jax import lax
+from jax.experimental import pallas as pl
+from jax.experimental.pallas import tpu as pltpu
 from jax.sharding import PartitionSpec as P
 
 KDEV = 8
@@ -105,6 +109,373 @@
     return (similarity, centroid)
 
 
+MESH = pl.DeviceIdType.MESH
+CHUNKS = 4
+BF = jnp.bfloat16
+F32 = jnp.float32
+
+
+def nt(a, b):
+    return lax.dot_general(a, b, (((1,), (1,)), ((), ())), preferred_element_type=F32)
+
+
+def mm(a, b):
+    return jnp.dot(a, b, preferred_element_type=F32)
+
+
+def row_to_column(row):
+    return jnp.broadcast_to(row, (128, row.shape[1])).T[:, :1]
+
+
+def fused_kernel(
+    sizes, emb_hbm, basis_hbm, label_ref, stamp_ref, sim_ref, cent_ref,
+    emb, own_basis, far_basis, place, half_out, half_in, outgoing, rows_in,
+    meta_out, meta_in, ret_out, ret_in, cent_out, cent_in,
+    emb_sem, basis_sem, x_send, x_recv, y_send, y_recv, sub_send, sub_recv,
+    meta_send, meta_recv, row_send, row_recv, ret_send, ret_recv,
+    cent_sem, local_sem,
+):
+    inner_n, sub_n, devices, slots = sizes
+    row_count = label_ref.shape[1]
+    g = lax.axis_index("groups")
+    o = lax.axis_index("owners")
+    i = lax.axis_index("inner")
+    s = lax.axis_index("sub")
+    chip = inner_n * sub_n
+    me = o * chip + i * sub_n + s
+    lane_base = (i * sub_n + s) * slots
+
+    def coordinates(t):
+        return (g, t // chip, (t // sub_n) % inner_n, t % sub_n)
+
+    x_peer = (g, o, 1 - i, s)
+    y_peer = (1 - g, o, i, s)
+    sub_peer = (g, o, i, 1 - s)
+    own_rows = pl.ds(pl.multiple_of(s * row_count, row_count), row_count)
+    far_rows = pl.ds(pl.multiple_of((1 - s) * row_count, row_count), row_count)
+
+    ret_in[...] = jnp.zeros_like(ret_in)
+    load_far = pltpu.make_async_copy(emb_hbm.at[far_rows], emb.at[far_rows], emb_sem.at[0])
+    load_own = pltpu.make_async_copy(emb_hbm.at[own_rows], emb.at[own_rows], emb_sem.at[1])
+    load_basis = pltpu.make_async_copy(basis_hbm, own_basis, basis_sem)
+    load_basis.start()
+    load_far.start()
+    load_own.start()
+
+    barrier = pltpu.get_barrier_semaphore()
+
+    def greet(j, carry):
+        pl.semaphore_signal(
+            barrier, inc=1, device_id=coordinates((me + j) % devices), device_id_type=MESH
+        )
+        return carry
+
+    lax.fori_loop(1, devices, greet, 0)
+    pl.semaphore_signal(barrier, inc=1, device_id=y_peer, device_id_type=MESH)
+    pl.semaphore_wait(barrier, devices)
+
+    depth = basis_hbm.shape[0]
+    piece = depth // 2 // CHUNKS
+
+    def span(group, c):
+        return pl.ds(pl.multiple_of(group * (depth // 2) + c * piece, piece), piece)
+
+    def x_copy(c):
+        return pltpu.make_async_remote_copy(
+            basis_hbm.at[span(g, c)], far_basis.at[span(g, c)],
+            x_send.at[c], x_recv.at[c], device_id=x_peer, device_id_type=MESH,
+        )
+
+    def y_copy(c):
+        return pltpu.make_async_remote_copy(
+            far_basis.at[span(g, c)], far_basis.at[span(g, c)],
+            y_send.at[c], y_recv.at[c], device_id=y_peer, device_id_type=MESH,
+        )
+
+    def y_arrival(c):
+        return pltpu.make_async_remote_copy(
+            far_basis.at[span(g, c)], far_basis.at[span(1 - g, c)],
+            y_send.at[c], y_recv.at[c], device_id=y_peer, device_id_type=MESH,
+        )
+
+    for c in range(CHUNKS):
+        x_copy(c).start()
+
+    labels = label_ref[...]
+    padded = (labels // 2) * 8 + labels % 2
+    up = lax.broadcasted_iota(jnp.int32, (128, row_count), 0)
+    member = up == padded
+    one_hot = jnp.where(member, 1.0, 0.0)
+    member_bf = one_hot.astype(BF)
+    earlier_row = lax.broadcasted_iota(jnp.int32, (row_count, row_count), 0) < (
+        lax.broadcasted_iota(jnp.int32, (row_count, row_count), 1)
+    )
+    before = mm(member_bf, jnp.where(earlier_row, 1.0, 0.0).astype(BF))
+    rank = jnp.sum(before * one_hot, axis=0, keepdims=True).astype(jnp.int32)
+    at_lane = up == rank + lane_base
+    lane_hot = jnp.where(at_lane, 1.0, 0.0).astype(BF)
+    coded = stamp_ref[...] + 1
+    meta = jnp.zeros((128, 128), F32)
+    for shift in (16, 8, 0):
+        digit = ((coded >> shift) & 255).astype(F32)
+        meta = meta + nt((one_hot * digit).astype(BF), lane_hot) * float(1 << shift)
+    meta_out[...] = meta.reshape(devices, 8, 128)
+    meta_in[me] = meta_out[me]
+
+    def meta_copy(j):
+        to = (me + j) % devices
+        return pltpu.make_async_remote_copy(
+            meta_out.at[to, pl.ds(0, 2)], meta_in.at[me, pl.ds(0, 2)],
+            meta_send.at[j], meta_recv.at[j], device_id=coordinates(to), device_id_type=MESH,
+        )
+
+    def start_meta(j, carry):
+        meta_copy(j).start()
+        return carry
+
+    lax.fori_loop(1, devices, start_meta, 0)
+    position = labels * slots + rank
+    place[...] = jnp.where(
+        lax.broadcasted_iota(jnp.int32, (place.shape[0], row_count), 0) == position, 1.0, 0.0
+    ).astype(BF)
+
+    def half_copy(h):
+        return pltpu.make_async_remote_copy(
+            half_out.at[h], half_in.at[h], sub_send.at[h], sub_recv.at[h],
+            device_id=sub_peer, device_id_type=MESH,
+        )
+
+    def column(h):
+        return pl.ds(pl.multiple_of((i if h == 0 else 1 - i) * 128, 128), 128)
+
+    my_slots = pl.ds(pl.multiple_of(me * slots, slots), slots)
+
+    def row_copy(h, j):
+        to = (me + j) % devices
+        return pltpu.make_async_remote_copy(
+            outgoing.at[h, pl.ds(to * 2, 2)], rows_in.at[:, my_slots, column(h)],
+            row_send.at[h, j], row_recv.at[h, j],
+            device_id=coordinates(to), device_id_type=MESH,
+        )
+
+    def own_copy(h):
+        return pltpu.make_async_copy(
+            outgoing.at[h, pl.ds(me * 2, 2)], rows_in.at[:, my_slots, column(h)], local_sem.at[h]
+        )
+
+    def send_half(h, own):
+        half_copy(h).wait_recv()
+        total = (own + half_in[h]).astype(BF)
+        outgoing[h] = mm(place[...], total).astype(BF).reshape(outgoing.shape[1:])
+
+        def start_rows(j, carry):
+            row_copy(h, j).start()
+            return carry
+
+        lax.fori_loop(1, devices, start_rows, 0)
+        own_copy(h).start()
+
+    load_basis.wait()
+    load_far.wait()
+    half_out[0] = mm(emb[far_rows, :], own_basis[...])
+    half_copy(0).start()
+    load_own.wait()
+    own = mm(emb[own_rows, :], own_basis[...])
+    for c in range(2):
+        x_copy(c).wait_recv()
+        y_copy(c).start()
+    send_half(0, own)
+    for c in range(2, CHUNKS):
+        x_copy(c).wait_recv()
+        y_copy(c).start()
+
+    for c in range(CHUNKS):
+        y_arrival(c).wait_recv()
+    half_out[1] = mm(emb[far_rows, :], far_basis[...])
+    half_copy(1).start()
+    own = mm(emb[own_rows, :], far_basis[...])
+    send_half(1, own)
+
+    for_meta = []
+
+    def wait_meta(j, carry):
+        meta_copy(j).wait_recv()
+        return carry
+
+    lax.fori_loop(1, devices, wait_meta, 0)
+    for k in range(2):
+        blocks = []
+        for b in range(devices // chip):
+            block = meta_in[b * chip, k:k + 1, :]
+            for q in range(1, chip):
+                block = block + meta_in[b * chip + q, k:k + 1, :]
+            blocks.append(block)
+        stamps = jnp.concatenate(blocks, axis=1)
+        stamps = jnp.where(stamps == 0.0, float(SENTINEL), stamps)
+        for_meta.append((stamps, row_to_column(stamps)))
+
+    def wait_rows(j, carry):
+        row_copy(0, j).wait_recv()
+        row_copy(1, j).wait_recv()
+        return carry
+
+    lax.fori_loop(1, devices, wait_rows, 0)
+    own_copy(0).wait()
+    own_copy(1).wait()
+
+    eye = lax.broadcasted_iota(jnp.int32, (128, 128), 0) == (
+        lax.broadcasted_iota(jnp.int32, (128, 128), 1)
+    )
+    ret_out[...] = jnp.zeros_like(ret_out)
+    inverses = []
+    for k in range(2):
+        keys = rows_in[k]
+        scores = nt(keys, keys)
+        blocks = [
+            jnp.sum(
+                jnp.where(eye, scores[b * 128:(b + 1) * 128, b * 128:(b + 1) * 128], 0.0),
+                axis=0, keepdims=True,
+            )
+            for b in range(scores.shape[0] // 128)
+        ]
+        inverse = lax.rsqrt(jnp.concatenate(blocks, axis=1) + EPS)
+        inverses.append(inverse)
+        stamps, stamp_column = for_meta[k]
+        scaled = scores * row_to_column(inverse)
+        best = jnp.max(jnp.where(stamp_column < stamps, scaled, -jnp.inf), axis=0, keepdims=True)
+        best = jnp.maximum(best * inverse, -1.0)
+        for b in range(devices // chip):
+            ret_out[b, k:k + 1, :] = best[:, b * 128:(b + 1) * 128]
+
+    def ret_copy(j):
+        to = (me + j) % devices
+        return pltpu.make_async_remote_copy(
+            ret_out.at[to // chip, pl.ds(0, 2)], ret_in.at[me, pl.ds(0, 2)],
+            ret_send.at[j], ret_recv.at[j], device_id=coordinates(to), device_id_type=MESH,
+        )
+
+    def start_ret(j, carry):
+        ret_copy(j).start()
+        return carry
+
+    lax.fori_loop(1, devices, start_ret, 0)
+    ret_in[me] = ret_out[o]
+
+    wide = rows_in.shape[2]
+    cents = []
+    for k in range(2):
+        high = inverses[k].astype(BF)
+        low = (inverses[k] - high.astype(F32)).astype(BF)
+        keys = rows_in[k]
+        fill = (8, inverses[k].shape[1])
+        sums = (
+            mm(jnp.broadcast_to(high, fill), keys) + mm(jnp.broadcast_to(low, fill), keys)
+        )[:1]
+        mean = jnp.sum(sums * sums, axis=1, keepdims=True) / wide
+        cents.append(sums * lax.rsqrt(mean + EPS))
+    cent_out[...] = jnp.zeros_like(cent_out)
+    for k in range(2):
+        left, right = cents[k][:, :128], cents[k][:, 128:]
+        cent_out[k:k + 1, :] = jnp.where(s == 0, right, left)
+    cent_copy = pltpu.make_async_remote_copy(
+        cent_out, cent_in, cent_sem.at[0], cent_sem.at[1],
+        device_id=sub_peer, device_id_type=MESH,
+    )
+    cent_copy.start()
+    cent_copy.wait_recv()
+    for k in range(2):
+        mine = jnp.where(s == 0, cents[k][:, :128], cents[k][:, 128:])
+        theirs = cent_in[k:k + 1, :]
+        cent_ref[k:k + 1, :] = jnp.where(s == 0, mine, theirs)
+        cent_ref[2 + k:3 + k, :] = jnp.where(s == 0, theirs, mine)
+
+    def wait_ret(j, carry):
+        ret_copy(j).wait_recv()
+        return carry
+
+    lax.fori_loop(1, devices, wait_ret, 0)
+    answers = ret_in[...].reshape(128, 128).T
+    picked = jnp.zeros((128, row_count), F32)
+    for _ in range(3):
+        part = answers.astype(BF)
+        picked = picked + mm(part, member_bf)
+        answers = answers - part.astype(F32)
+    sim_ref[...] = jnp.sum(jnp.where(at_lane, picked, 0.0), axis=0, keepdims=True)
+
+    def drain(j, carry):
+        meta_copy(j).wait_send()
+        row_copy(0, j).wait_send()
+        row_copy(1, j).wait_send()
+        ret_copy(j).wait_send()
+        return carry
+
+    lax.fori_loop(1, devices, drain, 0)
+    for c in range(CHUNKS):
+        x_copy(c).wait_send()
+        y_copy(c).wait_send()
+    for h in range(2):
+        half_copy(h).wait_send()
+    cent_copy.wait_send()
+
+
+def fused(embeddings, pca_basis, assignment, row_stamp):
+    row_count = assignment.shape[0]
+    owners_n = lax.axis_size("owners")
+    inner_n = lax.axis_size("inner")
+    sub_n = lax.axis_size("sub")
+    devices = owners_n * inner_n * sub_n
+    clusters = KDEV * owners_n
+    slots = 2 * row_count // clusters
+    depth, part = pca_basis.shape
+    wide = part * inner_n
+    dma = pltpu.SemaphoreType.DMA
+    hbm = pl.BlockSpec(memory_space=pl.ANY)
+    vmem = pl.BlockSpec(memory_space=pltpu.VMEM)
+    similarity, centroid = pl.pallas_call(
+        functools.partial(fused_kernel, (inner_n, sub_n, devices, slots)),
+        out_shape=(
+            jax.ShapeDtypeStruct((1, row_count), F32),
+            jax.ShapeDtypeStruct((KDEV // inner_n, wide // sub_n), F32),
+        ),
+        in_specs=[hbm, hbm, vmem, vmem],
+        out_specs=(vmem, vmem),
+        scratch_shapes=[
+            pltpu.VMEM(embeddings.shape, BF),
+            pltpu.VMEM((depth, part), BF),
+            pltpu.VMEM((depth, part), BF),
+            pltpu.VMEM((clusters * slots, row_count), BF),
+            pltpu.VMEM((2, row_count, part), F32),
+            pltpu.VMEM((2, row_count, part), F32),
+            pltpu.VMEM((2, clusters, slots, part), BF),
+            pltpu.VMEM((2, devices * slots, wide), BF),
+            pltpu.VMEM((devices, 8, 128), F32),
+            pltpu.VMEM((devices, 8, 128), F32),
+            pltpu.VMEM((owners_n, 8, 128), F32),
+            pltpu.VMEM((devices, 8, 128), F32),
+            pltpu.VMEM((8, 128), F32),
+            pltpu.VMEM((8, 128), F32),
+            dma((2,)), dma, dma((CHUNKS,)), dma((CHUNKS,)), dma((CHUNKS,)), dma((CHUNKS,)),
+            dma((2,)), dma((2,)),
+            dma((devices,)), dma((devices,)),
+            dma((2, devices)), dma((2, devices)),
+            dma((devices,)), dma((devices,)),
+            dma((2,)), dma((2,)),
+        ],
+        compiler_params=pltpu.CompilerParams(
+            collective_id=0, has_side_effects=True, vmem_limit_bytes=48 * 1024 * 1024
+        ),
+        cost_estimate=pl.CostEstimate(
+            flops=2 * embeddings.size * wide, bytes_accessed=2 * embeddings.size, transcendentals=0
+        ),
+    )(embeddings, pca_basis, assignment.reshape(1, row_count), row_stamp.reshape(1, row_count))
+    return similarity.reshape(row_count), centroid
+
+
+def fits(mesh):
+    size = mesh.shape
+    return (size["groups"], size["inner"], size["sub"], size["owners"]) == (2, 2, 2, 4)
+
+
 def solution(mesh):
     in_specs = (
         P(("groups", "owners", "inner"), "sub"),
@@ -114,5 +485,5 @@
     )
     out_specs = (P(("groups", "owners", "inner", "sub")), P(("groups", "owners", "inner"), "sub"))
     return jax.shard_map(
-        per_device, mesh=mesh, in_specs=in_specs, out_specs=out_specs, check_vma=False
-    )
+        fused if fits(mesh) else per_device, mesh=mesh, in_specs=in_specs, out_specs=out_specs, check_vma=False
+    )

time: 129 us -> 43.6 us (0.34)
  waiting for transfers between devices: 40.1 us -> 0 us
  Pallas kernels: 0 us -> 36.9 us
  blocking collectives: 34.6 us -> 0 us
  local copies, waits for them, and re-layouts: 22.3 us -> 5.74 us
  between operations: 14.6 us -> 0.65 us
  starting transfers between devices: 6.59 us -> 0 us
  matrix products: 5.64 us -> 0 us
  other arithmetic: 4.63 us -> 0 us
    pallas_call x0 -> x1, Pallas kernels: none -> 36.9 us  [fused(): pl.pallas_call(functools.partial(fused_kernel, (inner_n, sub_n, devices,...]
    all_gather x2 -> x0, waiting for transfers between devices: 25.6 us -> none  [the longest x1 25.6 us: per_device(): full_basis = lax.all_gather(pca_basis, 'inner', axis=1, tiled=True)]
    all_to_all x1 -> x0, blocking collectives: 19.7 us -> none  [per_device(): lax.all_to_all(outgoing.reshape(owners_n, KDEV * slot_count, features), '...]
    gather x3 -> x0, local copies, waits for them, and re-layouts: 16.1 us -> none  [the longest x1 8.77 us: per_device(): outgoing_stamp = padded_stamp[source]]
    all_to_all x2 -> x0, waiting for transfers between devices: 9.16 us -> none  [the longest x1 4.89 us: per_device(): lax.all_to_all(answer, 'owners', split_axis=0, concat_axis=0, tiled=True)]
    unnamed x1 -> x0, blocking collectives: 7.19 us -> none
    all_to_all x2 -> x0, starting transfers between devices: 6.48 us -> none  [the longest x1 3.24 us: per_device(): lax.all_to_all(answer, 'owners', split_axis=0, concat_axis=0, tiled=True)]
    dot_general x2 -> x0, matrix products: 5.64 us -> none  [the longest x1 4.73 us: per_device(): jnp.dot(embeddings, full_basis, preferred_element_type=jnp.float32)]
  transfers between devices with their start and end apart: 5 -> 0, of which waited for: 4 -> 0; matrix products, arithmetic and copies ran while one was open for 11% -> 0% of each run, Pallas kernels for 0% -> 0%
where the time goes in v1:
time: 43.6 us; the launch traced here: 43.3 us
  Pallas kernels  36.9 us (85%)
  local copies, waits for them, and re-layouts  5.74 us (13%)
  between operations  0.65 us (1%)
    pallas_call x1, Pallas kernels, fused(): pl.pallas_call(functools.partial(fused_kernel, (inner_n, sub_n, devices,...  36.9 us
    unnamed x10, local copies, waits for them, and re-layouts  5.74 us

profile of v1, /device:TPU:0, one launch (start us, length us, event | category | flops | bytes accessed | tf_op | source)
XLA Modules:
  0.0 43.3 jit_solution(12225367950948263234)
XLA Ops:
  0.6 0.0 copy-start
  0.6 2.2 %copy-done = bf16[1024,2048]{1,0:T(8,128)(2,1)S(1)} copy-done((bf16[1024,2048]{1,0:T(8,128)(2,1)S(1)}, bf16[1024,2048]{1,0:T(8,128)(2,1)}, u32[]{:S(2)}) %copy-start) | copy-done | bytes 4194328
  2.8 0.0 copy-start.1
  2.8 1.0 %copy-done.1 = bf16[2048,128]{1,0:T(8,128)(2,1)S(1)} copy-done((bf16[2048,128]{1,0:T(8,128)(2,1)S(1)}, bf16[2048,128]{1,0:T(8,128)(2,1)}, u32[]{:S(2)}) %copy-start.1) | copy-done | bytes 524312
  3.9 0.0 copy-start.2
  3.9 0.7 %copy-done.2 = s32[512,1]{0,1:T(1,128)S(1)} copy-done((s32[512,1]{0,1:T(1,128)S(1)}, s32[512,1]{0,1:T(1,128)}, u32[]{:S(2)}) %copy-start.2) | copy-done | bytes 2072
  4.5 0.0 copy-start.3
  4.5 0.7 %copy-done.3 = s32[512]{0:T(512)S(1)} copy-done((s32[512]{0:T(512)S(1)}, s32[512]{0:T(512)}, u32[]{:S(2)}) %copy-start.3) | copy-done | bytes 2072
  5.2 36.9 %shard_map.59 = (f32[1,512]{1,0:T(1,128)S(1)}, f32[4,128]{1,0:T(4,128)S(1)}) custom-call(bf16[1024,2048]{1,0:T(8,128)(2,1)S(1)} %copy-done, bf16[2048,128]{1,0:T(8,128)(2,1)S(1)} %copy-done.1, s32[1,512]{1,0:T(1,128)S(1)} %bitcast.3, s32[1,512]{1,0:T(1,128)S(1)} %bitcast.4), custom_call_target="tpu_custom_call" | custom-call | flops 1073741824 | bytes 4194304 | tf_op jit(solution)/shard_map/pallas_call | solution.py:434
  42.2 0.6 %copy.8 = f32[512]{0:T(512)} copy(f32[512]{0:T(512)S(1)} %bitcast.5) | data formatting | bytes 4096
  42.7 0.6 %copy.9 = f32[4,128]{1,0:T(4,128)} copy(f32[4,128]{1,0:T(4,128)S(1)} %get-tuple-element.9) | data formatting | bytes 4096
Async XLA Ops:
  0.6 2.2 %copy-start = (bf16[1024,2048]{1,0:T(8,128)(2,1)S(1)}, bf16[1024,2048]{1,0:T(8,128)(2,1)}, u32[]{:S(2)}) copy-start(bf16[1024,2048]{1,0:T(8,128)(2,1)} %emb_hbm.1) | copy-start | bytes 12582916
  2.8 1.0 %copy-start.1 = (bf16[2048,128]{1,0:T(8,128)(2,1)S(1)}, bf16[2048,128]{1,0:T(8,128)(2,1)}, u32[]{:S(2)}) copy-start(bf16[2048,128]{1,0:T(8,128)(2,1)} %basis_hbm.1) | copy-start | bytes 1572868
  3.9 0.7 %copy-start.2 = (s32[512,1]{0,1:T(1,128)S(1)}, s32[512,1]{0,1:T(1,128)}, u32[]{:S(2)}) copy-start(s32[512,1]{0,1:T(1,128)} %param.6) | copy-start | bytes 6148
  4.5 0.7 %copy-start.3 = (s32[512]{0:T(512)S(1)}, s32[512]{0:T(512)}, u32[]{:S(2)}) copy-start(s32[512]{0:T(512)} %param.7) | copy-start | bytes 6148

commit v2 on v1

--- a/solution.py
+++ b/solution.py
@@ -128,15 +128,15 @@
 
 
 def fused_kernel(
-    sizes, emb_hbm, basis_hbm, label_ref, stamp_ref, sim_ref, cent_ref,
+    sizes, emb_hbm, basis_hbm, label_hbm, stamp_hbm, sim_ref, cent_ref,
     emb, own_basis, far_basis, place, half_out, half_in, outgoing, rows_in,
     meta_out, meta_in, ret_out, ret_in, cent_out, cent_in,
     emb_sem, basis_sem, x_send, x_recv, y_send, y_recv, sub_send, sub_recv,
     meta_send, meta_recv, row_send, row_recv, ret_send, ret_recv,
-    cent_sem, local_sem,
+    cent_sem, local_sem, label_ref, stamp_ref,
 ):
     inner_n, sub_n, devices, slots = sizes
-    row_count = label_ref.shape[1]
+    row_count = label_hbm.shape[1]
     g = lax.axis_index("groups")
     o = lax.axis_index("owners")
     i = lax.axis_index("inner")
@@ -145,8 +145,15 @@
     me = o * chip + i * sub_n + s
     lane_base = (i * sub_n + s) * slots
 
-    def coordinates(t):
-        return (g, t // chip, (t // sub_n) % inner_n, t % sub_n)
+    owners_n = devices // chip
+    peers = []
+    for step in (2, 3, 1, 0):
+        owner = (o + step) % owners_n
+        for inner in (1 - i, i):
+            for sub in (1 - s, s):
+                if step or inner is not i or sub is not s:
+                    number = owner * chip + inner * sub_n + sub
+                    peers.append(((g, owner, inner, sub), owner, number))
 
     x_peer = (g, o, 1 - i, s)
     y_peer = (1 - g, o, i, s)
@@ -154,25 +161,22 @@
     own_rows = pl.ds(pl.multiple_of(s * row_count, row_count), row_count)
     far_rows = pl.ds(pl.multiple_of((1 - s) * row_count, row_count), row_count)
 
-    ret_in[...] = jnp.zeros_like(ret_in)
     load_far = pltpu.make_async_copy(emb_hbm.at[far_rows], emb.at[far_rows], emb_sem.at[0])
     load_own = pltpu.make_async_copy(emb_hbm.at[own_rows], emb.at[own_rows], emb_sem.at[1])
     load_basis = pltpu.make_async_copy(basis_hbm, own_basis, basis_sem)
+    load_labels = pltpu.make_async_copy(label_hbm, label_ref, local_sem.at[2])
+    load_stamps = pltpu.make_async_copy(stamp_hbm, stamp_ref, local_sem.at[3])
+    load_labels.start()
+    load_stamps.start()
     load_basis.start()
     load_far.start()
     load_own.start()
 
     barrier = pltpu.get_barrier_semaphore()
 
-    def greet(j, carry):
-        pl.semaphore_signal(
-            barrier, inc=1, device_id=coordinates((me + j) % devices), device_id_type=MESH
-        )
-        return carry
-
-    lax.fori_loop(1, devices, greet, 0)
-    pl.semaphore_signal(barrier, inc=1, device_id=y_peer, device_id_type=MESH)
-    pl.semaphore_wait(barrier, devices)
+    ret_in[...] = jnp.zeros_like(ret_in)
+    for target in [peer[0] for peer in peers] + [y_peer]:
+        pl.semaphore_signal(barrier, inc=1, device_id=target, device_id_type=MESH)
 
     depth = basis_hbm.shape[0]
     piece = depth // 2 // CHUNKS
@@ -198,9 +202,8 @@
             y_send.at[c], y_recv.at[c], device_id=y_peer, device_id_type=MESH,
         )
 
-    for c in range(CHUNKS):
-        x_copy(c).start()
-
+    load_labels.wait()
+    load_stamps.wait()
     labels = label_ref[...]
     padded = (labels // 2) * 8 + labels % 2
     up = lax.broadcasted_iota(jnp.int32, (128, row_count), 0)
@@ -222,18 +225,14 @@
     meta_out[...] = meta.reshape(devices, 8, 128)
     meta_in[me] = meta_out[me]
 
-    def meta_copy(j):
-        to = (me + j) % devices
-        return pltpu.make_async_remote_copy(
-            meta_out.at[to, pl.ds(0, 2)], meta_in.at[me, pl.ds(0, 2)],
-            meta_send.at[j], meta_recv.at[j], device_id=coordinates(to), device_id_type=MESH,
-        )
-
-    def start_meta(j, carry):
-        meta_copy(j).start()
-        return carry
-
-    lax.fori_loop(1, devices, start_meta, 0)
+    pl.semaphore_wait(barrier, devices)
+    for c in range(CHUNKS):
+        x_copy(c).start()
+    for target, owner, number in peers:
+        pltpu.make_async_remote_copy(
+            meta_out.at[number, pl.ds(0, 2)], meta_in.at[me, pl.ds(0, 2)],
+            meta_send, meta_recv, device_id=target, device_id_type=MESH,
+        ).start()
     position = labels * slots + rank
     place[...] = jnp.where(
         lax.broadcasted_iota(jnp.int32, (place.shape[0], row_count), 0) == position, 1.0, 0.0
@@ -250,13 +249,13 @@
 
     my_slots = pl.ds(pl.multiple_of(me * slots, slots), slots)
 
-    def row_copy(h, j):
-        to = (me + j) % devices
-        return pltpu.make_async_remote_copy(
-            outgoing.at[h, pl.ds(to * 2, 2)], rows_in.at[:, my_slots, column(h)],
-            row_send.at[h, j], row_recv.at[h, j],
-            device_id=coordinates(to), device_id_type=MESH,
-        )
+    def all_rows(sem):
+        part = outgoing.at[0, pl.ds(0, 2 * (devices - 1))]
+        return pltpu.make_async_copy(part, part, sem)
+
+    def all_small(sem):
+        part = meta_out.at[pl.ds(0, devices - 1), pl.ds(0, 2)]
+        return pltpu.make_async_copy(part, part, sem)
 
     def own_copy(h):
         return pltpu.make_async_copy(
@@ -268,11 +267,11 @@
         total = (own + half_in[h]).astype(BF)
         outgoing[h] = mm(place[...], total).astype(BF).reshape(outgoing.shape[1:])
 
-        def start_rows(j, carry):
-            row_copy(h, j).start()
-            return carry
-
-        lax.fori_loop(1, devices, start_rows, 0)
+        for target, owner, number in peers:
+            pltpu.make_async_remote_copy(
+                outgoing.at[h, pl.ds(number * 2, 2)], rows_in.at[:, my_slots, column(h)],
+                row_send.at[h], row_recv.at[h], device_id=target, device_id_type=MESH,
+            ).start()
         own_copy(h).start()
 
     load_basis.wait()
@@ -298,11 +297,7 @@
 
     for_meta = []
 
-    def wait_meta(j, carry):
-        meta_copy(j).wait_recv()
-        return carry
-
-    lax.fori_loop(1, devices, wait_meta, 0)
+    all_small(meta_recv).wait()
     for k in range(2):
         blocks = []
         for b in range(devices // chip):
@@ -314,12 +309,8 @@
         stamps = jnp.where(stamps == 0.0, float(SENTINEL), stamps)
         for_meta.append((stamps, row_to_column(stamps)))
 
-    def wait_rows(j, carry):
-        row_copy(0, j).wait_recv()
-        row_copy(1, j).wait_recv()
-        return carry
-
-    lax.fori_loop(1, devices, wait_rows, 0)
+    all_rows(row_recv.at[0]).wait()
+    all_rows(row_recv.at[1]).wait()
     own_copy(0).wait()
     own_copy(1).wait()
 
@@ -347,18 +338,11 @@
         for b in range(devices // chip):
             ret_out[b, k:k + 1, :] = best[:, b * 128:(b + 1) * 128]
 
-    def ret_copy(j):
-        to = (me + j) % devices
-        return pltpu.make_async_remote_copy(
-            ret_out.at[to // chip, pl.ds(0, 2)], ret_in.at[me, pl.ds(0, 2)],
-            ret_send.at[j], ret_recv.at[j], device_id=coordinates(to), device_id_type=MESH,
-        )
-
-    def start_ret(j, carry):
-        ret_copy(j).start()
-        return carry
-
-    lax.fori_loop(1, devices, start_ret, 0)
+    for target, owner, number in peers:
+        pltpu.make_async_remote_copy(
+            ret_out.at[owner, pl.ds(0, 2)], ret_in.at[me, pl.ds(0, 2)],
+            ret_send, ret_recv, device_id=target, device_id_type=MESH,
+        ).start()
     ret_in[me] = ret_out[o]
 
     wide = rows_in.shape[2]
@@ -389,11 +373,7 @@
         cent_ref[k:k + 1, :] = jnp.where(s == 0, mine, theirs)
         cent_ref[2 + k:3 + k, :] = jnp.where(s == 0, theirs, mine)
 
-    def wait_ret(j, carry):
-        ret_copy(j).wait_recv()
-        return carry
-
-    lax.fori_loop(1, devices, wait_ret, 0)
+    all_small(ret_recv).wait()
     answers = ret_in[...].reshape(128, 128).T
     picked = jnp.zeros((128, row_count), F32)
     for _ in range(3):
@@ -402,14 +382,10 @@
         answers = answers - part.astype(F32)
     sim_ref[...] = jnp.sum(jnp.where(at_lane, picked, 0.0), axis=0, keepdims=True)
 
-    def drain(j, carry):
-        meta_copy(j).wait_send()
-        row_copy(0, j).wait_send()
-        row_copy(1, j).wait_send()
-        ret_copy(j).wait_send()
-        return carry
-
-    lax.fori_loop(1, devices, drain, 0)
+    all_small(meta_send).wait()
+    all_small(ret_send).wait()
+    for h in range(2):
+        all_rows(row_send.at[h]).wait()
     for c in range(CHUNKS):
         x_copy(c).wait_send()
         y_copy(c).wait_send()
@@ -429,7 +405,7 @@
     depth, part = pca_basis.shape
     wide = part * inner_n
     dma = pltpu.SemaphoreType.DMA
-    hbm = pl.BlockSpec(memory_space=pl.ANY)
+    hbm = pl.BlockSpec(memory_space=pltpu.HBM)
     vmem = pl.BlockSpec(memory_space=pltpu.VMEM)
     similarity, centroid = pl.pallas_call(
         functools.partial(fused_kernel, (inner_n, sub_n, devices, slots)),
@@ -437,7 +413,7 @@
             jax.ShapeDtypeStruct((1, row_count), F32),
             jax.ShapeDtypeStruct((KDEV // inner_n, wide // sub_n), F32),
         ),
-        in_specs=[hbm, hbm, vmem, vmem],
+        in_specs=[hbm, hbm, hbm, hbm],
         out_specs=(vmem, vmem),
         scratch_shapes=[
             pltpu.VMEM(embeddings.shape, BF),
@@ -456,13 +432,13 @@
             pltpu.VMEM((8, 128), F32),
             dma((2,)), dma, dma((CHUNKS,)), dma((CHUNKS,)), dma((CHUNKS,)), dma((CHUNKS,)),
             dma((2,)), dma((2,)),
-            dma((devices,)), dma((devices,)),
-            dma((2, devices)), dma((2, devices)),
-            dma((devices,)), dma((devices,)),
-            dma((2,)), dma((2,)),
+            dma, dma, dma((2,)), dma((2,)), dma, dma,
+            dma((2,)), dma((4,)),
+            pltpu.VMEM((1, row_count), jnp.int32),
+            pltpu.VMEM((1, row_count), jnp.int32),
         ],
         compiler_params=pltpu.CompilerParams(
-            collective_id=0, has_side_effects=True, vmem_limit_bytes=48 * 1024 * 1024
+            collective_id=0, has_side_effects=True, vmem_limit_bytes=60 * 1024 * 1024
         ),
         cost_estimate=pl.CostEstimate(
             flops=2 * embeddings.size * wide, bytes_accessed=2 * embeddings.size, transcendentals=0

time: 43.6 us -> 38 us (0.87)
  local copies, waits for them, and re-layouts: 5.74 us -> 2.48 us
  Pallas kernels: 36.9 us -> 34.7 us
    unnamed x10 -> x2, local copies, waits for them, and re-layouts: 5.74 us -> 2.48 us
    pallas_call x1, Pallas kernels: 36.9 us -> 34.7 us  [fused(): pl.pallas_call(functools.partial(fused_kernel, (inner_n, sub_n, devices,...]
where the time goes in v2:
time: 38 us; the launch traced here: 37.8 us
  Pallas kernels  34.7 us (91%)
  local copies, waits for them, and re-layouts  2.48 us (7%)
  between operations  0.64 us (2%)
    pallas_call x1, Pallas kernels, fused(): pl.pallas_call(functools.partial(fused_kernel, (inner_n, sub_n, devices,...  34.7 us
    unnamed x2, local copies, waits for them, and re-layouts  2.48 us

profile of v2, /device:TPU:0, one launch (start us, length us, event | category | flops | bytes accessed | tf_op | source)
XLA Modules:
  0.0 37.8 jit_solution(1403527071066806266)
XLA Ops:
  0.6 34.7 %shard_map.59 = (f32[1,512]{1,0:T(1,128)}, f32[4,128]{1,0:T(4,128)}) custom-call(bf16[1024,2048]{1,0:T(8,128)(2,1)} %emb_hbm.1, bf16[2048,128]{1,0:T(8,128)(2,1)} %basis_hbm.1, s32[1,512]{1,0:T(1,128)} %bitcast.3, s32[1,512]{1,0:T(1,128)} %bitcast.4), custom_call_target="tpu_custom_call" | custom-call | flops 1073741824 | bytes 4194304 | tf_op jit(solution)/shard_map/pallas_call | solution.py:410
  35.3 1.2 %copy.8 = f32[512]{0:T(512)} copy(f32[512]{0:T(512)} %bitcast.5) | data formatting | bytes 4096
  36.6 1.2 %copy.9 = f32[4,128]{1,0:T(4,128)} copy(f32[4,128]{1,0:T(4,128)} %get-tuple-element.9) | data formatting | bytes 4096

commit v3 on v2

--- a/solution.py
+++ b/solution.py
@@ -111,6 +111,7 @@
 
 MESH = pl.DeviceIdType.MESH
 CHUNKS = 4
+BANDS = 2
 BF = jnp.bfloat16
 F32 = jnp.float32
 
@@ -133,7 +134,7 @@
     meta_out, meta_in, ret_out, ret_in, cent_out, cent_in,
     emb_sem, basis_sem, x_send, x_recv, y_send, y_recv, sub_send, sub_recv,
     meta_send, meta_recv, row_send, row_recv, ret_send, ret_recv,
-    cent_sem, local_sem, label_ref, stamp_ref,
+    cent_sem, local_sem, label_ref, stamp_ref, kept,
 ):
     inner_n, sub_n, devices, slots = sizes
     row_count = label_hbm.shape[1]
@@ -161,16 +162,27 @@
     own_rows = pl.ds(pl.multiple_of(s * row_count, row_count), row_count)
     far_rows = pl.ds(pl.multiple_of((1 - s) * row_count, row_count), row_count)
 
-    load_far = pltpu.make_async_copy(emb_hbm.at[far_rows], emb.at[far_rows], emb_sem.at[0])
-    load_own = pltpu.make_async_copy(emb_hbm.at[own_rows], emb.at[own_rows], emb_sem.at[1])
-    load_basis = pltpu.make_async_copy(basis_hbm, own_basis, basis_sem)
+    depth = basis_hbm.shape[0]
+    middle = depth // 2
+    spans = [pl.ds(pl.multiple_of(part * middle, middle), middle) for part in (g, 1 - g)]
+    load_far = [
+        pltpu.make_async_copy(emb_hbm.at[far_rows, spans[p]], emb.at[p, far_rows], emb_sem.at[p])
+        for p in range(2)
+    ]
+    load_own = [
+        pltpu.make_async_copy(emb_hbm.at[own_rows, spans[p]], emb.at[p, own_rows], emb_sem.at[2 + p])
+        for p in range(2)
+    ]
+    load_basis = [
+        pltpu.make_async_copy(basis_hbm.at[spans[p]], own_basis.at[p], basis_sem.at[p])
+        for p in range(2)
+    ]
     load_labels = pltpu.make_async_copy(label_hbm, label_ref, local_sem.at[2])
     load_stamps = pltpu.make_async_copy(stamp_hbm, stamp_ref, local_sem.at[3])
     load_labels.start()
     load_stamps.start()
-    load_basis.start()
-    load_far.start()
-    load_own.start()
+    for load in load_basis + load_far + load_own:
+        load.start()
 
     barrier = pltpu.get_barrier_semaphore()
 
@@ -178,27 +190,19 @@
     for target in [peer[0] for peer in peers] + [y_peer]:
         pl.semaphore_signal(barrier, inc=1, device_id=target, device_id_type=MESH)
 
-    depth = basis_hbm.shape[0]
-    piece = depth // 2 // CHUNKS
-
-    def span(group, c):
-        return pl.ds(pl.multiple_of(group * (depth // 2) + c * piece, piece), piece)
+    piece = middle // CHUNKS
 
     def x_copy(c):
+        rows = pl.ds(pl.multiple_of(g * middle + c * piece, piece), piece)
         return pltpu.make_async_remote_copy(
-            basis_hbm.at[span(g, c)], far_basis.at[span(g, c)],
+            basis_hbm.at[rows], far_basis.at[0, pl.ds(c * piece, piece)],
             x_send.at[c], x_recv.at[c], device_id=x_peer, device_id_type=MESH,
         )
 
     def y_copy(c):
+        rows = pl.ds(c * piece, piece)
         return pltpu.make_async_remote_copy(
-            far_basis.at[span(g, c)], far_basis.at[span(g, c)],
-            y_send.at[c], y_recv.at[c], device_id=y_peer, device_id_type=MESH,
-        )
-
-    def y_arrival(c):
-        return pltpu.make_async_remote_copy(
-            far_basis.at[span(g, c)], far_basis.at[span(1 - g, c)],
+            far_basis.at[0, rows], far_basis.at[1, rows],
             y_send.at[c], y_recv.at[c], device_id=y_peer, device_id_type=MESH,
         )
 
@@ -238,11 +242,18 @@
         lax.broadcasted_iota(jnp.int32, (place.shape[0], row_count), 0) == position, 1.0, 0.0
     ).astype(BF)
 
-    def half_copy(h):
+    band = row_count // BANDS
+
+    def half_copy(h, b):
+        rows = pl.ds(b * band, band)
         return pltpu.make_async_remote_copy(
-            half_out.at[h], half_in.at[h], sub_send.at[h], sub_recv.at[h],
+            half_out.at[h, rows], half_in.at[h, rows], sub_send.at[h, b], sub_recv.at[h, b],
             device_id=sub_peer, device_id_type=MESH,
         )
+
+    def far_band(b):
+        start = pl.multiple_of((1 - s) * row_count + b * band, band)
+        return pl.ds(start, band)
 
     def column(h):
         return pl.ds(pl.multiple_of((i if h == 0 else 1 - i) * 128, 128), 128)
@@ -263,10 +274,14 @@
         )
 
     def send_half(h, own):
-        half_copy(h).wait_recv()
+        for b in range(BANDS):
+            half_copy(h, b).wait_recv()
         total = (own + half_in[h]).astype(BF)
         outgoing[h] = mm(place[...], total).astype(BF).reshape(outgoing.shape[1:])
 
+        if h == 0:
+            x_copy(2).wait_recv()
+            y_copy(2).start()
         for target, owner, number in peers:
             pltpu.make_async_remote_copy(
                 outgoing.at[h, pl.ds(number * 2, 2)], rows_in.at[:, my_slots, column(h)],
@@ -274,25 +289,32 @@
             ).start()
         own_copy(h).start()
 
-    load_basis.wait()
-    load_far.wait()
-    half_out[0] = mm(emb[far_rows, :], own_basis[...])
-    half_copy(0).start()
-    load_own.wait()
-    own = mm(emb[own_rows, :], own_basis[...])
+    for load in load_basis + load_far:
+        load.wait()
+    for b in range(BANDS):
+        half_out[0, b * band:(b + 1) * band] = (
+            mm(emb[0, far_band(b), :], own_basis[0]) + mm(emb[1, far_band(b), :], own_basis[1])
+        )
+        half_copy(0, b).start()
+    for load in load_own:
+        load.wait()
+    own = mm(emb[0, own_rows, :], own_basis[0]) + mm(emb[1, own_rows, :], own_basis[1])
     for c in range(2):
         x_copy(c).wait_recv()
         y_copy(c).start()
     send_half(0, own)
-    for c in range(2, CHUNKS):
+    for c in range(3, CHUNKS):
         x_copy(c).wait_recv()
         y_copy(c).start()
 
+    half_out[1] = mm(emb[0, far_rows, :], far_basis[0])
+    kept[...] = mm(emb[0, own_rows, :], far_basis[0])
     for c in range(CHUNKS):
-        y_arrival(c).wait_recv()
-    half_out[1] = mm(emb[far_rows, :], far_basis[...])
-    half_copy(1).start()
-    own = mm(emb[own_rows, :], far_basis[...])
+        y_copy(c).wait_recv()
+    for b in range(BANDS):
+        half_out[1, b * band:(b + 1) * band] += mm(emb[1, far_band(b), :], far_basis[1])
+        half_copy(1, b).start()
+    own = kept[...] + mm(emb[1, own_rows, :], far_basis[1])
     send_half(1, own)
 
     for_meta = []
@@ -366,13 +388,6 @@
         device_id=sub_peer, device_id_type=MESH,
     )
     cent_copy.start()
-    cent_copy.wait_recv()
-    for k in range(2):
-        mine = jnp.where(s == 0, cents[k][:, :128], cents[k][:, 128:])
-        theirs = cent_in[k:k + 1, :]
-        cent_ref[k:k + 1, :] = jnp.where(s == 0, mine, theirs)
-        cent_ref[2 + k:3 + k, :] = jnp.where(s == 0, theirs, mine)
-
     all_small(ret_recv).wait()
     answers = ret_in[...].reshape(128, 128).T
     picked = jnp.zeros((128, row_count), F32)
@@ -382,6 +397,17 @@
         answers = answers - part.astype(F32)
     sim_ref[...] = jnp.sum(jnp.where(at_lane, picked, 0.0), axis=0, keepdims=True)
 
+    cent_copy.wait_recv()
+    mine = jnp.concatenate(
+        [jnp.where(s == 0, cents[k][:, :128], cents[k][:, 128:]) for k in range(2)], axis=0
+    )
+    theirs = cent_in[0:2, :]
+    cent_ref[...] = jnp.where(
+        s == 0,
+        jnp.concatenate([mine, theirs], axis=0),
+        jnp.concatenate([theirs, mine], axis=0),
+    )
+
     all_small(meta_send).wait()
     all_small(ret_send).wait()
     for h in range(2):
@@ -390,7 +416,8 @@
         x_copy(c).wait_send()
         y_copy(c).wait_send()
     for h in range(2):
-        half_copy(h).wait_send()
+        for b in range(BANDS):
+            half_copy(h, b).wait_send()
     cent_copy.wait_send()
 
 
@@ -416,9 +443,9 @@
         in_specs=[hbm, hbm, hbm, hbm],
         out_specs=(vmem, vmem),
         scratch_shapes=[
-            pltpu.VMEM(embeddings.shape, BF),
-            pltpu.VMEM((depth, part), BF),
-            pltpu.VMEM((depth, part), BF),
+            pltpu.VMEM((2, embeddings.shape[0], depth // 2), BF),
+            pltpu.VMEM((2, depth // 2, part), BF),
+            pltpu.VMEM((2, depth // 2, part), BF),
             pltpu.VMEM((clusters * slots, row_count), BF),
             pltpu.VMEM((2, row_count, part), F32),
             pltpu.VMEM((2, row_count, part), F32),
@@ -430,12 +457,13 @@
             pltpu.VMEM((devices, 8, 128), F32),
             pltpu.VMEM((8, 128), F32),
             pltpu.VMEM((8, 128), F32),
-            dma((2,)), dma, dma((CHUNKS,)), dma((CHUNKS,)), dma((CHUNKS,)), dma((CHUNKS,)),
-            dma((2,)), dma((2,)),
+            dma((4,)), dma((2,)), dma((CHUNKS,)), dma((CHUNKS,)), dma((CHUNKS,)), dma((CHUNKS,)),
+            dma((2, BANDS)), dma((2, BANDS)),
             dma, dma, dma((2,)), dma((2,)), dma, dma,
             dma((2,)), dma((4,)),
             pltpu.VMEM((1, row_count), jnp.int32),
             pltpu.VMEM((1, row_count), jnp.int32),
+            pltpu.VMEM((row_count, part), F32),
         ],
         compiler_params=pltpu.CompilerParams(
             collective_id=0, has_side_effects=True, vmem_limit_bytes=60 * 1024 * 1024

time: 38 us -> 36.5 us (0.961)
  Pallas kernels: 34.7 us -> 33.1 us
    pallas_call x1, Pallas kernels: 34.7 us -> 33.1 us  [fused(): pl.pallas_call(functools.partial(fused_kernel, (inner_n, sub_n, devices,...]
where the time goes in v3:
time: 36.5 us; the launch traced here: 36.3 us
  Pallas kernels  33.1 us (91%)
  local copies, waits for them, and re-layouts  2.48 us (7%)
  between operations  0.64 us (2%)
    pallas_call x1, Pallas kernels, fused(): pl.pallas_call(functools.partial(fused_kernel, (inner_n, sub_n, devices,...  33.1 us
    unnamed x2, local copies, waits for them, and re-layouts  2.48 us

profile of v3, /device:TPU:0, one launch (start us, length us, event | category | flops | bytes accessed | tf_op | source)
XLA Modules:
  0.0 36.3 jit_solution(17729417316485037996)
XLA Ops:
  0.6 33.1 %shard_map.59 = (f32[1,512]{1,0:T(1,128)}, f32[4,128]{1,0:T(4,128)}) custom-call(bf16[1024,2048]{1,0:T(8,128)(2,1)} %emb_hbm.1, bf16[2048,128]{1,0:T(8,128)(2,1)} %basis_hbm.1, s32[1,512]{1,0:T(1,128)} %bitcast.3, s32[1,512]{1,0:T(1,128)} %bitcast.4), custom_call_target="tpu_custom_call" | custom-call | flops 1073741824 | bytes 4194304 | tf_op jit(solution)/shard_map/pallas_call | solution.py:437
  33.8 1.2 %copy.8 = f32[512]{0:T(512)} copy(f32[512]{0:T(512)} %bitcast.5) | data formatting | bytes 4096
  35.0 1.2 %copy.9 = f32[4,128]{1,0:T(4,128)} copy(f32[4,128]{1,0:T(4,128)} %get-tuple-element.9) | data formatting | bytes 4096
